TPU v7x, 32 devices: a whole 2x2x4 slice. The times are simulated.
32 devices in a mesh: slot: 4 (over y, core), asset: 8 (over z, x).
Axes of the slice: x: 2, y: 2, z: 4, core: 2. Of those that a mesh axis runs over, the one named last changes fastest.
Arguments:
- slot_emb: bfloat16 [8192, 768], P(('slot', 'asset')), may hold values from -4 to 4
- asset_panel: bfloat16 [768, 8192], P('slot', 'asset'), may hold values from -4 to 4
- mult: int32 [8192], P('slot'), may hold values from 1 to 4
- caps: int32 [8192], P('asset'), may hold values from 1 to 8, as said below
Outputs:
- plan: float32 [8192, 8192], P('slot', 'asset')
Inputs may be any that keep to these rules, and one draw needn't show every extreme that they name: caps are whole numbers; the last asset's cap is the largest.
All inputs are finite; a program needn't handle non-finite values.
Results may differ from a plain program's by a relative error of at most 0.0003.
Values may be sent and summed in bfloat16 or wider, within the bound.
A program may use at most 64 MiB of HBM per device.

v0:
```python
import jax
import jax.numpy as jnp
from jax import lax
from jax.sharding import PartitionSpec as P

EMB = 768
ITERS = 3


def combined_all(value, axis, join):
    pieces = jax.tree.map(lambda part: lax.all_gather(part, axis), value)
    head = jax.tree.map(lambda part: part[0], pieces)
    tail = jax.tree.map(lambda part: part[1:], pieces)
    so_far, _ = lax.scan(lambda so_far, share: (join(so_far, share), None), head, tail)
    return so_far


def combine_lse(first, second):
    peak = jnp.maximum(first[0], second[0])
    total = first[1] * jnp.exp(first[0] - peak) + second[1] * jnp.exp(second[0] - peak)
    return (peak, total)


def row_side(logits, asset_pot):
    shifted = logits + asset_pot[None, :]
    peak = lax.pmax(jnp.max(shifted, axis=1), "asset")
    total = lax.psum(jnp.sum(jnp.exp(shifted - peak[:, None]), axis=1), "asset")
    return peak + jnp.log(total)


def col_side(logits, slot_pot):
    shifted = logits + slot_pot[:, None]
    local_peak = jnp.max(shifted, axis=0)
    local_total = jnp.sum(jnp.exp(shifted - local_peak[None, :]), axis=0)
    peak, total = combined_all((local_peak, local_total), "slot", combine_lse)
    return peak + jnp.log(total)


def per_device(slot_emb, asset_panel, mult, caps):
    slot_block = lax.all_gather(slot_emb, "asset", axis=0, tiled=True)
    logits = jnp.dot(
        slot_block,
        lax.all_gather(asset_panel, "slot", axis=0, tiled=True),
        preferred_element_type=jnp.float32,
    ) * EMB ** (-0.5)
    caps_float = caps.astype(jnp.float32)
    cap_total = lax.psum(jnp.sum(caps_float), "asset")
    log_b = jnp.log(caps_float) - jnp.log(cap_total)
    log_a = jnp.log(mult.astype(jnp.float32))
    asset_pot = jnp.zeros((logits.shape[1],), jnp.float32)
    slot_pot = jnp.zeros((logits.shape[0],), jnp.float32)
    for iteration in range(ITERS):
        slot_pot = log_a - row_side(logits, asset_pot)
        asset_pot = log_b - col_side(logits, slot_pot)
    factor = float(
        logits.shape[0] * lax.axis_size("slot") * logits.shape[1] * lax.axis_size("asset")
    )
    return jnp.exp(logits + slot_pot[:, None] + asset_pot[None, :]) * factor


def solution(mesh):
    return jax.shard_map(
        per_device,
        mesh=mesh,
        in_specs=(P(("slot", "asset"), None), P("slot", "asset"), P("slot"), P("asset")),
        out_specs=P("slot", "asset"),
        check_vma=False,
    )
```

profile of v0, /device:TPU:0, one launch (start us, length us, event | category | flops | bytes accessed | tf_op | source)
XLA Modules:
  0.0 306.0 jit_solution(16252835963483229316)
XLA Ops:
  9.3 22.0 %all-gather.11.cloned.1.call-done = bf16[768,1024]{1,0:T(8,128)(2,1)} async-done(((bf16[192,1024]{1,0:T(8,128)(2,1)}), bf16[768,1024]{1,0:T(8,128)(2,1)}) %all-gather.11.cloned.1.call-update) | async-done | bytes 1572880 | tf_op jit(solution)/shard_map/all_gather | solution.py:43
  31.3 62.7 %all-gather.9.cloned.1.call-done = bf16[2048,768]{1,0:T(8,128)(2,1)} async-done(((bf16[256,768]{1,0:T(8,128)(2,1)}), bf16[2048,768]{1,0:T(8,128)(2,1)}) %all-gather.9.cloned.1.call-update) | async-done | bytes 3145744 | tf_op jit(solution)/shard_map/all_gather | solution.py:40
  94.0 9.2 %fusion = (f32[2048]{0:T(1024)S(1)}, f32[2048,1024]{1,0:T(8,128)}) fusion(bf16[2048,768]{1,0:T(8,128)(2,1)} %all-gather.9.cloned.1.call-done, bf16[768,1024]{1,0:T(8,128)(2,1)} %all-gather.11.cloned.1.call-done), kind=kOutput, calls=%fused_computation.31 | convolution fusion | flops 3225417728 | bytes 13115392 | tf_op jit(solution)/shard_map/dot_general | solution.py:41
  103.2 19.3 %pmax.21 = f32[2048]{0:T(1024)S(1)} all-reduce(f32[2048]{0:T(1024)S(1)} %get-tuple-element.139), channel_id=1, replica_groups=mesh['slot'=4,'asset'=8] {'asset'}, use_global_device_ids=true, to_apply=%region_3.0 | all-reduce | flops 2048 | bytes 16384 | tf_op jit(solution)/shard_map/pmax | solution.py:26
  122.5 4.4 %exponential_reduce_fusion.5 = f32[2048]{0:T(1024)S(1)} fusion(f32[2048,1024]{1,0:T(8,128)} %get-tuple-element.140, f32[2048]{0:T(1024)S(1)} %pmax.21), kind=kLoop, calls=%fused_computation.15 | loop fusion | flops 4192256 | bytes 8404992 | tf_op jit(solution)/shard_map/reduce_sum | solution.py:27
  126.9 18.3 %all-reduce = (f32[2048]{0:T(1024)S(1)}, f32[]{:T(128)}) all-reduce(f32[2048]{0:T(1024)S(1)} %exponential_reduce_fusion.5, f32[]{:T(128)} %convert_reduce_fusion), channel_id=1, replica_groups=mesh['slot'=4,'asset'=8] {'asset'}, use_global_device_ids=true, to_apply=%region_5.0 | all-reduce | flops 2049 | bytes 16392 | tf_op jit(solution)/shard_map/psum | solution.py:27
  149.2 4.2 %exponential_reduce_fusion.4 = f32[1024]{0:T(1024)S(1)} fusion(f32[2048,1024]{1,0:T(8,128)} %get-tuple-element.140, f32[1024]{0:T(1024)S(1)} %add_reduce_fusion.3, f32[2048]{0:T(1024)S(1)} %add_subtract_fusion.2), kind=kLoop, calls=%fused_computation.14 | loop fusion | flops 6290432 | bytes 8404992 | tf_op jit(solution)/shard_map/reduce_sum | solution.py:34
  153.4 5.2 %all-gather = f32[4096]{0:T(1024)S(1)} all-gather(f32[1024]{0:T(1024)S(1)} %add_reduce_fusion.3), channel_id=2, replica_groups=mesh['slot'=4,'asset'=8] {'slot'}, dimensions={0}, use_global_device_ids=true | all-gather | bytes 20480 | tf_op jit(solution)/shard_map/all_gather | solution.py:11
  158.6 5.2 %all-gather.1 = f32[4096]{0:T(1024)S(1)} all-gather(f32[1024]{0:T(1024)S(1)} %exponential_reduce_fusion.4), channel_id=3, replica_groups=mesh['slot'=4,'asset'=8] {'slot'}, dimensions={0}, use_global_device_ids=true | all-gather | bytes 20480 | tf_op jit(solution)/shard_map/all_gather | solution.py:11
  164.6 4.0 %add_reduce_fusion.2 = f32[2048]{0:T(1024)S(1)} fusion(f32[2048,1024]{1,0:T(8,128)} %get-tuple-element.140, f32[1024]{0:T(1024)S(1)} %add_subtract_fusion.5), kind=kLoop, calls=%fused_computation.18 | loop fusion | flops 4192256 | bytes 8400896 | tf_op jit(solution)/shard_map/reduce_max | solution.py:26
  168.6 19.4 %pmax.22 = f32[2048]{0:T(1024)S(1)} all-reduce(f32[2048]{0:T(1024)S(1)} %add_reduce_fusion.2), channel_id=1, replica_groups=mesh['slot'=4,'asset'=8] {'asset'}, use_global_device_ids=true, to_apply=%region_11.12 | all-reduce | flops 2048 | bytes 16384 | tf_op jit(solution)/shard_map/pmax | solution.py:26
  188.0 4.4 %exponential_reduce_fusion.3 = f32[2048]{0:T(1024)S(1)} fusion(f32[2048,1024]{1,0:T(8,128)} %get-tuple-element.140, f32[2048]{0:T(1024)S(1)} %pmax.22, f32[1024]{0:T(1024)S(1)} %add_subtract_fusion.5), kind=kLoop, calls=%fused_computation.13 | loop fusion | flops 6289408 | bytes 8409088 | tf_op jit(solution)/shard_map/reduce_sum | solution.py:27
  192.4 17.4 %psum.30 = f32[2048]{0:T(1024)S(1)} all-reduce(f32[2048]{0:T(1024)S(1)} %exponential_reduce_fusion.3), channel_id=1, replica_groups=mesh['slot'=4,'asset'=8] {'asset'}, use_global_device_ids=true, to_apply=%region_13.14 | all-reduce | flops 2048 | bytes 16384 | tf_op jit(solution)/shard_map/psum | solution.py:27
  213.8 4.2 %exponential_reduce_fusion.2 = f32[1024]{0:T(1024)S(1)} fusion(f32[2048,1024]{1,0:T(8,128)} %get-tuple-element.140, f32[1024]{0:T(1024)S(1)} %add_reduce_fusion.1, f32[2048]{0:T(1024)S(1)} %add_subtract_fusion.1), kind=kLoop, calls=%fused_computation.12 | loop fusion | flops 6290432 | bytes 8404992 | tf_op jit(solution)/shard_map/reduce_sum | solution.py:34
  218.1 5.2 %all-gather.2 = f32[4096]{0:T(1024)S(1)} all-gather(f32[1024]{0:T(1024)S(1)} %add_reduce_fusion.1), channel_id=4, replica_groups=mesh['slot'=4,'asset'=8] {'slot'}, dimensions={0}, use_global_device_ids=true | all-gather | bytes 20480 | tf_op jit(solution)/shard_map/all_gather | solution.py:11
  223.3 5.2 %all-gather.3 = f32[4096]{0:T(1024)S(1)} all-gather(f32[1024]{0:T(1024)S(1)} %exponential_reduce_fusion.2), channel_id=5, replica_groups=mesh['slot'=4,'asset'=8] {'slot'}, dimensions={0}, use_global_device_ids=true | all-gather | bytes 20480 | tf_op jit(solution)/shard_map/all_gather | solution.py:11
  228.6 4.0 %add_reduce_fusion = f32[2048]{0:T(1024)S(1)} fusion(f32[2048,1024]{1,0:T(8,128)} %get-tuple-element.140, f32[1024]{0:T(1024)S(1)} %add_subtract_fusion.4), kind=kLoop, calls=%fused_computation.16 | loop fusion | flops 4192256 | bytes 8400896 | tf_op jit(solution)/shard_map/reduce_max | solution.py:26
  232.7 19.4 %pmax.23 = f32[2048]{0:T(1024)S(1)} all-reduce(f32[2048]{0:T(1024)S(1)} %add_reduce_fusion), channel_id=1, replica_groups=mesh['slot'=4,'asset'=8] {'asset'}, use_global_device_ids=true, to_apply=%region_19.20 | all-reduce | flops 2048 | bytes 16384 | tf_op jit(solution)/shard_map/pmax | solution.py:26
  252.1 4.4 %exponential_reduce_fusion.1 = f32[2048]{0:T(1024)S(1)} fusion(f32[2048,1024]{1,0:T(8,128)} %get-tuple-element.140, f32[2048]{0:T(1024)S(1)} %pmax.23, f32[1024]{0:T(1024)S(1)} %add_subtract_fusion.4), kind=kLoop, calls=%fused_computation.11 | loop fusion | flops 6289408 | bytes 8409088 | tf_op jit(solution)/shard_map/reduce_sum | solution.py:27
  256.4 17.6 %psum.31 = f32[2048]{0:T(1024)S(1)} all-reduce(f32[2048]{0:T(1024)S(1)} %exponential_reduce_fusion.1), channel_id=1, replica_groups=mesh['slot'=4,'asset'=8] {'asset'}, use_global_device_ids=true, to_apply=%region_21.22 | all-reduce | flops 2048 | bytes 16384 | tf_op jit(solution)/shard_map/psum | solution.py:27
  278.0 4.2 %exponential_reduce_fusion = f32[1024]{0:T(1024)S(1)} fusion(f32[2048,1024]{1,0:T(8,128)} %get-tuple-element.140, f32[1024]{0:T(1024)S(1)} %add_reduce_fusion.4, f32[2048]{0:T(1024)S(1)} %add_subtract_fusion), kind=kLoop, calls=%fused_computation.10 | loop fusion | flops 6290432 | bytes 8404992 | tf_op jit(solution)/shard_map/reduce_sum | solution.py:34
  282.3 5.2 %all-gather.4 = f32[4096]{0:T(1024)S(1)} all-gather(f32[1024]{0:T(1024)S(1)} %add_reduce_fusion.4), channel_id=6, replica_groups=mesh['slot'=4,'asset'=8] {'slot'}, dimensions={0}, use_global_device_ids=true | all-gather | bytes 20480 | tf_op jit(solution)/shard_map/all_gather | solution.py:11
  287.5 5.2 %all-gather.5 = f32[4096]{0:T(1024)S(1)} all-gather(f32[1024]{0:T(1024)S(1)} %exponential_reduce_fusion), channel_id=7, replica_groups=mesh['slot'=4,'asset'=8] {'slot'}, dimensions={0}, use_global_device_ids=true | all-gather | bytes 20480 | tf_op jit(solution)/shard_map/all_gather | solution.py:11
  292.8 6.3 %exponential_multiply_fusion = f32[2048,1024]{1,0:T(8,128)} fusion(f32[2048,1024]{1,0:T(8,128)} %get-tuple-element.140, f32[1024]{0:T(1024)S(1)} %add_subtract_fusion.3, f32[2048]{0:T(1024)S(1)} %add_subtract_fusion), kind=kLoop, calls=%fused_computation.9 | loop fusion | flops 6291456 | bytes 16789504 | tf_op jit(solution)/shard_map/mul | solution.py:58
  (57 shorter events, 15.6 us)
Async XLA Ops:
  6.5 24.8 %all-gather.11.cloned.1.call-start = ((), (), s32[]{:S(2)}) async-start(), calls=%async_computation.1 | async-start | bytes 1966080 | tf_op jit(solution)/shard_map/all_gather | solution.py:43
  7.3 86.7 %all-gather.9.cloned.1.call-start = ((), (), s32[]{:S(2)}) async-start(), calls=%async_computation | async-start | bytes 3538944 | tf_op jit(solution)/shard_map/all_gather | solution.py:40
  103.2 42.0 %copy-start = (s32[2048]{0:T(1024)S(1)}, s32[2048]{0:T(1024)}, u32[]{:S(2)}) copy-start(s32[2048]{0:T(1024)} %param.12) | copy-start | bytes 24580
  145.2 19.4 %copy-start.1 = (s32[1024]{0:T(1024)S(1)}, s32[1024]{0:T(1024)}, u32[]{:S(2)}) copy-start(s32[1024]{0:T(1024)} %param.13) | copy-start | bytes 12292
Sparse Core Ops, SparseCore 0:
  8.9 22.3 all-gather.10
  33.5 60.4 all-gather.8
where the time goes:
time: 307 us; the launch traced here: 306 us
  blocking collectives  142 us (46%)
  waiting for transfers between devices  86.1 us (28%)
  other arithmetic  53.6 us (17%)
  between operations  14.2 us (5%)
  matrix products  9.19 us (3%)
    all_gather x1, waiting for transfers between devices, per_device(): slot_block = lax.all_gather(slot_emb, 'asset', axis=0, tiled=True)  62.7 us
    pmax x3, blocking collectives, row_side(): peak = lax.pmax(jnp.max(shifted, axis=1), 'asset')  58.1 us
    psum x3, blocking collectives, row_side(): total = lax.psum(jnp.sum(jnp.exp(shifted - peak[:, None]), axis=1), 'asset')  53.2 us
    all_gather x6, blocking collectives, combined_all(): pieces = jax.tree.map(lambda part: lax.all_gather(part, axis), value)  31.1 us
    all_gather x1, waiting for transfers between devices, per_device(): lax.all_gather(asset_panel, 'slot', axis=0, tiled=True)  22 us
    reduce_sum x3, other arithmetic, row_side(): total = lax.psum(jnp.sum(jnp.exp(shifted - peak[:, None]), axis=1), 'asset')  13.1 us
    reduce_sum x3, other arithmetic, col_side(): local_total = jnp.sum(jnp.exp(shifted - local_peak[None, :]), axis=0)  12.7 us
    reduce_max x3, other arithmetic, col_side(): local_peak = jnp.max(shifted, axis=0)  12 us
  transfers between devices with their start and end apart: 2, of which 2 were waited for; matrix products, arithmetic and copies ran while one was open for 0% of the time, Pallas kernels for 0%

commit v1 on v0

v1 whole, which is shorter than its diff:
```python
import functools

import jax
import jax.numpy as jnp
from jax import lax
from jax.experimental import pallas as pl
from jax.experimental.pallas import tpu as pltpu
from jax.sharding import PartitionSpec as P

EMB = 768
ITERS = 3
LANES = 128
MESH = pl.DeviceIdType.MESH


def ring_spot(index, n):
    side = lax.rem(index, 2)
    up = lax.div(index, 2)
    return (1 - side) * up + side * (n - 1 - up)


def ring_index(spot, n):
    side = lax.div(spot, n // 2)
    return (1 - side) * (2 * spot) + side * (2 * (n - 1 - spot) + 1)


def loop(count, body, start=0):
    def step(i, carry):
        body(i)
        return carry

    lax.fori_loop(start, count, step, 0)


def kernel(ns, na, x_ref, w_ref, mult_ref, caps_ref, out_ref, sp_ref, ap_ref,
           xg, wg, lg, peak_ref, total_ref, spread, rbuf, cbuf, kbuf,
           rs, rr, ls, lr, ws, wr, es, er, fs, fr, ks, kr, osem):
    ms, ma = lax.axis_index("slot"), lax.axis_index("asset")
    block, depth = x_ref.shape[0], w_ref.shape[0]
    half = block // 2
    rows, cols = lg.shape
    tiles = cols // LANES
    bands = rows // LANES

    barrier = pltpu.get_barrier_semaphore()
    loop(ns, lambda d: pl.semaphore_signal(
        barrier, inc=1, device_id=(lax.rem(ms + d, ns), ma), device_id_type=MESH), 1)
    loop(na, lambda d: pl.semaphore_signal(
        barrier, inc=1, device_id=(ms, lax.rem(ma + d, na)), device_id_type=MESH), 1)

    def x_rows(spot, lower):
        return pl.ds(pl.multiple_of(ring_index(spot, na) * block + lower * half, half), half)

    def w_rows(owner):
        return pl.ds(pl.multiple_of(owner * depth, depth), depth)

    here = ring_spot(ma, na)
    right = ring_index(lax.rem(here + 1, na), na)
    left = ring_index(lax.rem(here + na - 1, na), na)
    xg[pl.ds(pl.multiple_of(ma * block, block), block), :] = x_ref[...]
    wg[w_rows(ms), :] = w_ref[...]
    caps = caps_ref[...].astype(jnp.float32)
    kbuf[ma] = jnp.broadcast_to(
        jnp.sum(jnp.sum(caps, axis=0, keepdims=True), axis=1, keepdims=True), (8, LANES))
    pl.semaphore_wait(barrier, ns + na - 2)

    def to_right(s):
        part = xg.at[x_rows(lax.rem(here + na - s, na), 0), :]
        return pltpu.make_async_remote_copy(
            src_ref=part, dst_ref=part, send_sem=rs.at[s], recv_sem=rr.at[s],
            device_id=(ms, right), device_id_type=MESH)

    def to_left(s):
        part = xg.at[x_rows(lax.rem(here + s, na), 1), :]
        return pltpu.make_async_remote_copy(
            src_ref=part, dst_ref=part, send_sem=ls.at[s], recv_sem=lr.at[s],
            device_id=(ms, left), device_id_type=MESH)

    def from_left(s):
        part = xg.at[x_rows(lax.rem(here + na - s - 1, na), 0), :]
        return pltpu.make_async_remote_copy(
            src_ref=part, dst_ref=part, send_sem=rs.at[s], recv_sem=rr.at[s],
            device_id=(ms, right), device_id_type=MESH)

    def from_right(s):
        part = xg.at[x_rows(lax.rem(here + s + 1, na), 1), :]
        return pltpu.make_async_remote_copy(
            src_ref=part, dst_ref=part, send_sem=ls.at[s], recv_sem=lr.at[s],
            device_id=(ms, left), device_id_type=MESH)

    def panel(d, owner):
        part = wg.at[w_rows(owner), :]
        return pltpu.make_async_remote_copy(
            src_ref=part, dst_ref=part, send_sem=ws.at[d], recv_sem=wr.at[d],
            device_id=(lax.rem(ms + d, ns), ma), device_id_type=MESH)

    def swap(buf, send, recv, slot, n, axis_slot):
        me = ms if axis_slot else ma

        def copy(d, owner):
            peer = lax.rem(me + d, n)
            part = buf.at[(slot, owner) if slot is not None else (owner,)]
            k = (slot, d) if slot is not None else (d,)
            return pltpu.make_async_remote_copy(
                src_ref=part, dst_ref=part, send_sem=send.at[k], recv_sem=recv.at[k],
                device_id=(peer, ma) if axis_slot else (ms, peer), device_id_type=MESH)

        def start():
            loop(n, lambda d: copy(d, me).start(), 1)

        def finish():
            loop(n, lambda d: copy(d, lax.rem(me + n - d, n)).wait_recv(), 1)
            loop(n, lambda d: copy(d, me).wait_send(), 1)

        return start, finish

    def product(t):
        for spot, lower in ((lax.rem(here + na - t, na), 0), (lax.rem(here + t, na), 1)):
            part = x_rows(spot, lower)
            lg[part, :] = jnp.dot(
                xg[part, :], wg[...], preferred_element_type=jnp.float32) * EMB ** (-0.5)

    def hop(s):
        from_left(s).wait_recv()
        from_right(s).wait_recv()

        @pl.when(s + 1 < na - 1)
        def _():
            to_right(s + 1).start()
            to_left(s + 1).start()

    to_right(0).start()
    to_left(0).start()
    loop(ns, lambda d: panel(d, ms).start(), 1)
    caps_start, caps_finish = swap(kbuf, ks, kr, None, na, False)
    caps_start()

    early = na // 2
    loop(early, hop)
    loop(ns, lambda d: panel(d, lax.rem(ms + ns - d, ns)).wait_recv(), 1)

    def late(u):
        hop(early + u)
        product(2 * u)
        product(2 * u + 1)

    loop(na - 1 - early, late)
    loop(na, product, 2 * (na - 1 - early))

    out = pltpu.make_async_copy(lg, out_ref, osem)
    out.start()

    caps_finish()
    log_b = jnp.log(caps) - jnp.log(jnp.sum(kbuf[...], axis=0)[0:1, :])
    log_a = jnp.log(mult_ref[...].astype(jnp.float32))
    ap_ref[...] = jnp.zeros_like(ap_ref)

    rchunk = 32
    cchunk = 64

    def lanes(k):
        return slice(k * LANES, (k + 1) * LANES)

    def join(parts):
        peak = jnp.max(parts, axis=0)
        return peak + jnp.log(jnp.sum(jnp.exp(parts - peak[None]), axis=0))

    for it in range(ITERS):
        def row_step(i):
            r = pl.ds(pl.multiple_of(i * rchunk, rchunk), rchunk)
            shifted = [lg[r, lanes(k)] + ap_ref[k:k + 1, :] for k in range(tiles)]
            peak = functools.reduce(jnp.maximum, shifted)
            peak_ref[r, :] = peak
            total_ref[r, :] = functools.reduce(jnp.add, [jnp.exp(v - peak) for v in shifted])

        loop(rows // rchunk, row_step)
        for b in range(bands):
            peaks = peak_ref[b * LANES:(b + 1) * LANES, :].T
            totals = total_ref[b * LANES:(b + 1) * LANES, :].T
            peak = jnp.max(peaks, axis=0, keepdims=True)
            total = jnp.sum(totals * jnp.exp(peaks - peak), axis=0, keepdims=True)
            rbuf[it, ma, b:b + 1, :] = peak + jnp.log(total)
        start, finish = swap(rbuf, es, er, it, na, False)
        start()
        finish()
        sp_ref[...] = log_a - join(rbuf[it])
        for b in range(bands):
            spread[b * LANES:(b + 1) * LANES, :] = jnp.broadcast_to(
                sp_ref[b:b + 1, :], (LANES, LANES)).T

        for k in range(tiles):
            def col_step(i, carry):
                peak, total = carry
                r = pl.ds(pl.multiple_of(i * cchunk, cchunk), cchunk)
                shifted = (lg[r, lanes(k)] + spread[r, :]).reshape(cchunk // 8, 8, LANES)
                fresh = jnp.maximum(peak, jnp.max(shifted, axis=0))
                total = total * jnp.exp(peak - fresh) + jnp.sum(
                    jnp.exp(shifted - fresh[None]), axis=0)
                return fresh, total

            init = (jnp.full((8, LANES), -jnp.inf, jnp.float32), jnp.zeros((8, LANES), jnp.float32))
            peaks, totals = lax.fori_loop(0, rows // cchunk, col_step, init, unroll=2)
            peak = jnp.max(peaks, axis=0, keepdims=True)
            total = jnp.sum(totals * jnp.exp(peaks - peak), axis=0, keepdims=True)
            cbuf[it, ms, k:k + 1, :] = peak + jnp.log(total)
        start, finish = swap(cbuf, fs, fr, it, ns, True)
        start()
        finish()
        ap_ref[...] = log_b - join(cbuf[it])

    def drain(s):
        to_right(s).wait_send()
        to_left(s).wait_send()

    loop(na - 1, drain)
    loop(ns, lambda d: panel(d, ms).wait_send(), 1)
    out.wait()


def per_device(ns, na, slot_emb, asset_panel, mult, caps):
    rows, cols = mult.shape[0], caps.shape[0]
    bands, tiles = rows // LANES, cols // LANES
    vmem = pl.BlockSpec(memory_space=pltpu.VMEM)
    dma = pltpu.SemaphoreType.DMA
    f32 = jnp.float32
    logits, slot_pot, asset_pot = pl.pallas_call(
        functools.partial(kernel, ns, na),
        out_shape=(
            jax.ShapeDtypeStruct((rows, cols), f32),
            jax.ShapeDtypeStruct((bands, LANES), f32),
            jax.ShapeDtypeStruct((tiles, LANES), f32),
        ),
        in_specs=[vmem] * 4,
        out_specs=(pl.BlockSpec(memory_space=pl.ANY), vmem, vmem),
        scratch_shapes=[
            pltpu.VMEM((rows, EMB), jnp.bfloat16),
            pltpu.VMEM((EMB, cols), jnp.bfloat16),
            pltpu.VMEM((rows, cols), f32),
            pltpu.VMEM((rows, LANES), f32),
            pltpu.VMEM((rows, LANES), f32),
            pltpu.VMEM((rows, LANES), f32),
            pltpu.VMEM((ITERS, na, bands, LANES), f32),
            pltpu.VMEM((ITERS, ns, tiles, LANES), f32),
            pltpu.VMEM((na, 8, LANES), f32),
            dma((na,)), dma((na,)), dma((na,)), dma((na,)),
            dma((ns,)), dma((ns,)),
            dma((ITERS, na)), dma((ITERS, na)),
            dma((ITERS, ns)), dma((ITERS, ns)),
            dma((na,)), dma((na,)),
            dma,
        ],
        compiler_params=pltpu.CompilerParams(
            collective_id=0, has_side_effects=True, vmem_limit_bytes=40 * 2**20),
    )(slot_emb, asset_panel, mult.reshape(bands, LANES), caps.reshape(tiles, LANES))
    factor = float(rows * ns * cols * na)
    return jnp.exp(
        logits + slot_pot.reshape(rows)[:, None] + asset_pot.reshape(cols)[None, :]) * factor


def solution(mesh):
    return jax.shard_map(
        functools.partial(per_device, mesh.shape["slot"], mesh.shape["asset"]),
        mesh=mesh,
        in_specs=(P(("slot", "asset"), None), P("slot", "asset"), P("slot"), P("asset")),
        out_specs=P("slot", "asset"),
        check_vma=False,
    )
```

time: 307 us -> 103 us (0.34)
  blocking collectives: 142 us -> 0 us
  Pallas kernels: 0 us -> 95.4 us
  waiting for transfers between devices: 86.1 us -> 0 us
  other arithmetic: 53.6 us -> 4.17 us
  between operations: 14.2 us -> 0.01 us
  matrix products: 9.19 us -> 0 us
  local copies, waits for them, and re-layouts: 0.2 us -> 3.37 us
    pallas_call x0 -> x1, Pallas kernels: none -> 95.4 us  [per_device(): pl.pallas_call(functools.partial(kernel, ns, na), out_shape=(jax.ShapeDty...]
    all_gather x2 -> x0, waiting for transfers between devices: 84.7 us -> none  [the longest x1 62.7 us: per_device(): slot_block = lax.all_gather(slot_emb, 'asset', axis=0, tiled=True)]
    pmax x3 -> x0, blocking collectives: 58.1 us -> none  [row_side(): peak = lax.pmax(jnp.max(shifted, axis=1), 'asset')]
    psum x3 -> x0, blocking collectives: 53.2 us -> none  [row_side(): total = lax.psum(jnp.sum(jnp.exp(shifted - peak[:, None]), axis=1), 'asset')]
    all_gather x6 -> x0, blocking collectives: 31.1 us -> none  [combined_all(): pieces = jax.tree.map(lambda part: lax.all_gather(part, axis), value)]
    reduce_sum x7 -> x0, other arithmetic: 27.1 us -> none  [the longest x3 13.1 us: row_side(): total = lax.psum(jnp.sum(jnp.exp(shifted - peak[:, None]), axis=1), 'asset')]
    reduce_max x5 -> x0, other arithmetic: 20 us -> none  [the longest x3 12 us: col_side(): local_peak = jnp.max(shifted, axis=0)]
    dot_general x1 -> x0, matrix products: 9.19 us -> none  [per_device(): jnp.dot(slot_block, lax.all_gather(asset_panel, 'slot', axis=0, tiled=Tru...]
  transfers between devices with their start and end apart: 2 -> 0, of which waited for: 2 -> 0; matrix products, arithmetic and copies ran while one was open for 0% -> 0% of each run, Pallas kernels for 0% -> 0%
where the time goes in v1:
time: 103 us
  Pallas kernels  95.4 us (93%)
  other arithmetic  4.17 us (4%)
  local copies, waits for them, and re-layouts  3.37 us (3%)
    pallas_call x1, Pallas kernels, per_device(): pl.pallas_call(functools.partial(kernel, ns, na), out_shape=(jax.ShapeDty...  95.4 us
    mul x1, other arithmetic, per_device(): jnp.exp(logits + slot_pot.reshape(rows)[:, None] + asset_pot.reshape(cols...  4.17 us
    unnamed x8, local copies, waits for them, and re-layouts  3.37 us

profile of v1, /device:TPU:0, one launch (start us, length us, event | category | flops | bytes accessed | tf_op | source)
XLA Modules:
  0.0 103.0 jit_solution(5607028041390680054)
XLA Ops:
  0.0 0.0 copy-start
  0.0 1.0 copy-done
  1.0 0.0 copy-start.1
  1.0 1.0 copy-done.1
  2.0 0.0 copy-start.2
  2.0 0.7 copy-done.2
  2.7 0.0 copy-start.3
  2.7 0.7 copy-done.3
  3.4 95.4 %shard_map.46 = (f32[2048,1024]{1,0:T(8,128)S(1)}, f32[16,128]{1,0:T(8,128)S(1)}, f32[8,128]{1,0:T(8,128)S(1)}) custom-call(bf16[256,768]{1,0:T(8,128)(2,1)S(1)} %copy-done, bf16[192,1024]{1,0:T(8,128)(2,1)S(1)} %copy-done.1, s32[16,128]{1,0:T(8,128)S(1)} %bitcast.4, s32[8,128]{1,0:T(8,128)S(1)} %bitcast.6), custom_call_target="tpu_custom_call" | custom-call | tf_op jit(solution)/shard_map/pallas_call | solution.py:226
  98.8 4.2 %exponential_multiply_fusion = f32[2048,1024]{1,0:T(8,128)} fusion(f32[2048,1024]{1,0:T(8,128)S(1)} %get-tuple-element.8, f32[1024]{0:T(1024)S(1)} %bitcast.7, f32[2048]{0:T(1024)S(1)} %bitcast.5), kind=kLoop, calls=%fused_computation | loop fusion | flops 6291456 | bytes 16789504 | tf_op jit(solution)/shard_map/mul | solution.py:256
Async XLA Ops:
  0.0 1.0 copy-start
  1.0 1.0 copy-start.1
  2.0 0.7 copy-start.2
  2.7 0.7 copy-start.3

commit v2 on v1

--- a/solution.py
+++ b/solution.py
@@ -1,4 +1,5 @@
 import functools
+import math
 
 import jax
 import jax.numpy as jnp
@@ -9,6 +10,7 @@
 
 EMB = 768
 ITERS = 3
+SCALE = EMB ** (-0.5) * math.log2(math.e)
 LANES = 128
 MESH = pl.DeviceIdType.MESH
 
@@ -34,7 +36,8 @@
 
 def kernel(ns, na, x_ref, w_ref, mult_ref, caps_ref, out_ref, sp_ref, ap_ref,
            xg, wg, lg, peak_ref, total_ref, spread, rbuf, cbuf, kbuf,
-           rs, rr, ls, lr, ws, wr, es, er, fs, fr, ks, kr, osem):
+           rs, rr, ls, lr, ws, wr, es, er, fs, fr, ks, kr, osem,
+           isem, caps_own, mult_own):
     ms, ma = lax.axis_index("slot"), lax.axis_index("asset")
     block, depth = x_ref.shape[0], w_ref.shape[0]
     half = block // 2
@@ -57,9 +60,18 @@
     here = ring_spot(ma, na)
     right = ring_index(lax.rem(here + 1, na), na)
     left = ring_index(lax.rem(here + na - 1, na), na)
-    xg[pl.ds(pl.multiple_of(ma * block, block), block), :] = x_ref[...]
-    wg[w_rows(ms), :] = w_ref[...]
-    caps = caps_ref[...].astype(jnp.float32)
+    loads = [
+        pltpu.make_async_copy(x_ref, xg.at[pl.ds(pl.multiple_of(ma * block, block), block), :], isem.at[0]),
+        pltpu.make_async_copy(w_ref, wg.at[w_rows(ms), :], isem.at[1]),
+        pltpu.make_async_copy(caps_ref, caps_own, isem.at[2]),
+        pltpu.make_async_copy(mult_ref, mult_own, isem.at[3]),
+    ]
+    for load in loads:
+        load.start()
+    ap_ref[...] = jnp.zeros_like(ap_ref)
+    for load in loads:
+        load.wait()
+    caps = caps_own[...].astype(jnp.float32)
     kbuf[ma] = jnp.broadcast_to(
         jnp.sum(jnp.sum(caps, axis=0, keepdims=True), axis=1, keepdims=True), (8, LANES))
     pl.semaphore_wait(barrier, ns + na - 2)
@@ -93,6 +105,8 @@
         return pltpu.make_async_remote_copy(
             src_ref=part, dst_ref=part, send_sem=ws.at[d], recv_sem=wr.at[d],
             device_id=(lax.rem(ms + d, ns), ma), device_id_type=MESH)
+
+    sent = []
 
     def swap(buf, send, recv, slot, n, axis_slot):
         me = ms if axis_slot else ma
@@ -110,23 +124,43 @@
 
         def finish():
             loop(n, lambda d: copy(d, lax.rem(me + n - d, n)).wait_recv(), 1)
-            loop(n, lambda d: copy(d, me).wait_send(), 1)
+            sent.append(lambda: loop(n, lambda d: copy(d, me).wait_send(), 1))
 
         return start, finish
+
+    rchunk = 32
+    cchunk = 128
+
+    def lanes(k):
+        return slice(k * LANES, (k + 1) * LANES)
+
+    def row_step(first):
+        r = pl.ds(first, rchunk)
+        shifted = [lg[r, lanes(k)] + ap_ref[k:k + 1, :] for k in range(tiles)]
+        peak = functools.reduce(jnp.maximum, shifted)
+        peak_ref[r, :] = peak
+        total_ref[r, :] = functools.reduce(jnp.add, [jnp.exp2(v - peak) for v in shifted])
 
     def product(t):
         for spot, lower in ((lax.rem(here + na - t, na), 0), (lax.rem(here + t, na), 1)):
             part = x_rows(spot, lower)
             lg[part, :] = jnp.dot(
-                xg[part, :], wg[...], preferred_element_type=jnp.float32) * EMB ** (-0.5)
+                xg[part, :], wg[...], preferred_element_type=jnp.float32) * SCALE
+            first = ring_index(spot, na) * block + lower * half
+            for j in range(half // rchunk):
+                row_step(pl.multiple_of(first + j * rchunk, rchunk))
 
     def hop(s):
         from_left(s).wait_recv()
-        from_right(s).wait_recv()
 
         @pl.when(s + 1 < na - 1)
         def _():
             to_right(s + 1).start()
+
+        from_right(s).wait_recv()
+
+        @pl.when(s + 1 < na - 1)
+        def _():
             to_left(s + 1).start()
 
     to_right(0).start()
@@ -151,35 +185,26 @@
     out.start()
 
     caps_finish()
-    log_b = jnp.log(caps) - jnp.log(jnp.sum(kbuf[...], axis=0)[0:1, :])
-    log_a = jnp.log(mult_ref[...].astype(jnp.float32))
-    ap_ref[...] = jnp.zeros_like(ap_ref)
-
-    rchunk = 32
-    cchunk = 64
-
-    def lanes(k):
-        return slice(k * LANES, (k + 1) * LANES)
+    log_b = jnp.log2(caps) - jnp.log2(jnp.sum(kbuf[...], axis=0)[0:1, :])
+    log_a = jnp.log2(mult_own[...].astype(jnp.float32))
 
     def join(parts):
         peak = jnp.max(parts, axis=0)
-        return peak + jnp.log(jnp.sum(jnp.exp(parts - peak[None]), axis=0))
+        return peak + jnp.log2(jnp.sum(jnp.exp2(parts - peak[None]), axis=0))
 
     for it in range(ITERS):
-        def row_step(i):
-            r = pl.ds(pl.multiple_of(i * rchunk, rchunk), rchunk)
-            shifted = [lg[r, lanes(k)] + ap_ref[k:k + 1, :] for k in range(tiles)]
-            peak = functools.reduce(jnp.maximum, shifted)
-            peak_ref[r, :] = peak
-            total_ref[r, :] = functools.reduce(jnp.add, [jnp.exp(v - peak) for v in shifted])
-
-        loop(rows // rchunk, row_step)
+        if it:
+            def row_pair(i):
+                for j in range(2):
+                    row_step(pl.multiple_of((2 * i + j) * rchunk, rchunk))
+
+            loop(rows // (2 * rchunk), row_pair)
         for b in range(bands):
             peaks = peak_ref[b * LANES:(b + 1) * LANES, :].T
             totals = total_ref[b * LANES:(b + 1) * LANES, :].T
             peak = jnp.max(peaks, axis=0, keepdims=True)
-            total = jnp.sum(totals * jnp.exp(peaks - peak), axis=0, keepdims=True)
-            rbuf[it, ma, b:b + 1, :] = peak + jnp.log(total)
+            total = jnp.sum(totals * jnp.exp2(peaks - peak), axis=0, keepdims=True)
+            rbuf[it, ma, b:b + 1, :] = peak + jnp.log2(total)
         start, finish = swap(rbuf, es, er, it, na, False)
         start()
         finish()
@@ -188,21 +213,25 @@
             spread[b * LANES:(b + 1) * LANES, :] = jnp.broadcast_to(
                 sp_ref[b:b + 1, :], (LANES, LANES)).T
 
-        for k in range(tiles):
+        for k in range(0, tiles, 2):
             def col_step(i, carry):
-                peak, total = carry
                 r = pl.ds(pl.multiple_of(i * cchunk, cchunk), cchunk)
-                shifted = (lg[r, lanes(k)] + spread[r, :]).reshape(cchunk // 8, 8, LANES)
-                fresh = jnp.maximum(peak, jnp.max(shifted, axis=0))
-                total = total * jnp.exp(peak - fresh) + jnp.sum(
-                    jnp.exp(shifted - fresh[None]), axis=0)
-                return fresh, total
+                pots = spread[r, :]
+                result = []
+                for j, (peak, total) in enumerate(carry):
+                    shifted = (lg[r, lanes(k + j)] + pots).reshape(cchunk // 8, 8, LANES)
+                    fresh = jnp.maximum(peak, jnp.max(shifted, axis=0))
+                    total = total * jnp.exp2(peak - fresh) + jnp.sum(
+                        jnp.exp2(shifted - fresh[None]), axis=0)
+                    result.append((fresh, total))
+                return tuple(result)
 
             init = (jnp.full((8, LANES), -jnp.inf, jnp.float32), jnp.zeros((8, LANES), jnp.float32))
-            peaks, totals = lax.fori_loop(0, rows // cchunk, col_step, init, unroll=2)
-            peak = jnp.max(peaks, axis=0, keepdims=True)
-            total = jnp.sum(totals * jnp.exp(peaks - peak), axis=0, keepdims=True)
-            cbuf[it, ms, k:k + 1, :] = peak + jnp.log(total)
+            done = lax.fori_loop(0, rows // cchunk, col_step, (init, init))
+            for j, (peaks, totals) in enumerate(done):
+                peak = jnp.max(peaks, axis=0, keepdims=True)
+                total = jnp.sum(totals * jnp.exp2(peaks - peak), axis=0, keepdims=True)
+                cbuf[it, ms, k + j:k + j + 1, :] = peak + jnp.log2(total)
         start, finish = swap(cbuf, fs, fr, it, ns, True)
         start()
         finish()
@@ -213,6 +242,8 @@
         to_left(s).wait_send()
 
     loop(na - 1, drain)
+    for wait in sent:
+        wait()
     loop(ns, lambda d: panel(d, ms).wait_send(), 1)
     out.wait()
 
@@ -230,7 +261,7 @@
             jax.ShapeDtypeStruct((bands, LANES), f32),
             jax.ShapeDtypeStruct((tiles, LANES), f32),
         ),
-        in_specs=[vmem] * 4,
+        in_specs=[pl.BlockSpec(memory_space=pltpu.HBM)] * 4,
         out_specs=(pl.BlockSpec(memory_space=pl.ANY), vmem, vmem),
         scratch_shapes=[
             pltpu.VMEM((rows, EMB), jnp.bfloat16),
@@ -248,12 +279,15 @@
             dma((ITERS, ns)), dma((ITERS, ns)),
             dma((na,)), dma((na,)),
             dma,
+            dma((4,)),
+            pltpu.VMEM((tiles, LANES), jnp.int32),
+            pltpu.VMEM((bands, LANES), jnp.int32),
         ],
         compiler_params=pltpu.CompilerParams(
             collective_id=0, has_side_effects=True, vmem_limit_bytes=40 * 2**20),
     )(slot_emb, asset_panel, mult.reshape(bands, LANES), caps.reshape(tiles, LANES))
     factor = float(rows * ns * cols * na)
-    return jnp.exp(
+    return jnp.exp2(
         logits + slot_pot.reshape(rows)[:, None] + asset_pot.reshape(cols)[None, :]) * factor
 
 

time: 103 us -> 95.8 us (0.930)
  Pallas kernels: 95.4 us -> 87.9 us
    pallas_call x1, Pallas kernels: 95.4 us -> 87.9 us  [per_device(): pl.pallas_call(functools.partial(kernel, ns, na), out_shape=(jax.ShapeDty...]
where the time goes in v2:
time: 95.8 us; the launch traced here: 95.6 us
  Pallas kernels  87.9 us (92%)
  other arithmetic  4.31 us (4%)
  local copies, waits for them, and re-layouts  3.37 us (4%)
    pallas_call x1, Pallas kernels, per_device(): pl.pallas_call(functools.partial(kernel, ns, na), out_shape=(jax.ShapeDty...  87.9 us
    mul x1, other arithmetic, per_device(): jnp.exp2(logits + slot_pot.reshape(rows)[:, None] + asset_pot.reshape(col...  4.31 us
    unnamed x8, local copies, waits for them, and re-layouts  3.37 us

profile of v2, /device:TPU:0, one launch (start us, length us, event | category | flops | bytes accessed | tf_op | source)
XLA Modules:
  0.0 95.6 jit_solution(16921737344063256472)
XLA Ops:
  0.0 0.0 copy-start
  0.0 1.0 %copy-done = bf16[256,768]{1,0:T(8,128)(2,1)S(1)} copy-done((bf16[256,768]{1,0:T(8,128)(2,1)S(1)}, bf16[256,768]{1,0:T(8,128)(2,1)}, u32[]{:S(2)}) %copy-start) | copy-done | bytes 393240
  1.0 0.0 copy-start.1
  1.0 1.0 %copy-done.1 = bf16[192,1024]{1,0:T(8,128)(2,1)S(1)} copy-done((bf16[192,1024]{1,0:T(8,128)(2,1)S(1)}, bf16[192,1024]{1,0:T(8,128)(2,1)}, u32[]{:S(2)}) %copy-start.1) | copy-done | bytes 393240
  2.0 0.0 copy-start.2
  2.0 0.7 copy-done.2
  2.7 0.0 copy-start.3
  2.7 0.7 copy-done.3
  3.4 87.9 %shard_map.46 = (f32[2048,1024]{1,0:T(8,128)S(1)}, f32[16,128]{1,0:T(8,128)S(1)}, f32[8,128]{1,0:T(8,128)S(1)}) custom-call(bf16[256,768]{1,0:T(8,128)(2,1)S(1)} %copy-done, bf16[192,1024]{1,0:T(8,128)(2,1)S(1)} %copy-done.1, s32[16,128]{1,0:T(8,128)S(1)} %bitcast.4, s32[8,128]{1,0:T(8,128)S(1)} %bitcast.6), custom_call_target="tpu_custom_call" | custom-call | tf_op jit(solution)/shard_map/pallas_call | solution.py:257
  91.3 4.3 %exponential_multiply_fusion = f32[2048,1024]{1,0:T(8,128)} fusion(f32[2048,1024]{1,0:T(8,128)S(1)} %get-tuple-element.8, f32[1024]{0:T(1024)S(1)} %bitcast.7, f32[2048]{0:T(1024)S(1)} %bitcast.5), kind=kLoop, calls=%fused_computation | loop fusion | flops 8388608 | bytes 16789504 | tf_op jit(solution)/shard_map/mul | solution.py:290
Async XLA Ops:
  0.0 1.0 %copy-start = (bf16[256,768]{1,0:T(8,128)(2,1)S(1)}, bf16[256,768]{1,0:T(8,128)(2,1)}, u32[]{:S(2)}) copy-start(bf16[256,768]{1,0:T(8,128)(2,1)} %x_ref.1) | copy-start | bytes 1179652
  1.0 1.0 %copy-start.1 = (bf16[192,1024]{1,0:T(8,128)(2,1)S(1)}, bf16[192,1024]{1,0:T(8,128)(2,1)}, u32[]{:S(2)}) copy-start(bf16[192,1024]{1,0:T(8,128)(2,1)} %w_ref.1) | copy-start | bytes 1179652
  2.0 0.7 copy-start.2
  2.7 0.7 copy-start.3
